TPU v7x, 32 devices: a whole 2x2x4 slice. The times are simulated.
32 devices in a mesh: dp: 8 (over y, x, core), mp: 4 (over z).
Axes of the slice: x: 2, y: 2, z: 4, core: 2. Of those that a mesh axis runs over, the one named last changes fastest.
Arguments:
- clean_image: bfloat16 [4, 588, 128], P('mp'), may hold values from -6 to 6
- noise_draw: bfloat16 [4, 8, 588, 128], P('mp', 'dp'), may hold values from -6 to 6
- embed_weight: bfloat16 [588, 6144], P(None, 'dp'), may hold values from -0.25 to 0.25
- position_table: bfloat16 [128, 6144], replicated, may hold values from -3 to 3
- norm_gain: float32 [6144], replicated, may hold values from 0.1 to 1.9
- qkv_weight: bfloat16 [6144, 3, 3072], P(None, None, 'mp'), may hold values from -0.078125 to 0.078125
- query_gain: float32 [128], replicated, may hold values from 0.1 to 1.9
- key_gain: float32 [128], replicated, may hold values from 0.1 to 1.9
- out_weight: bfloat16 [3072, 6144], P('mp'), may hold values from -0.375 to 0.375
Outputs:
- features: bfloat16 [128, 8, 4, 6144], P(None, 'dp', 'mp')
- smoothed: float32 [128, 4, 6144], P(None, 'mp', 'dp')
All inputs are finite; a program needn't handle non-finite values.
Results may differ from a plain program's by a relative error of at most 0.017.
Values may be sent and summed in bfloat16 or wider, within the bound.
A program may use at most 128 MiB of HBM per device.

v0:
```python
import jax
import jax.numpy as jnp
from jax import lax
from jax.sharding import PartitionSpec as P

HEAD_DIM = 128


epsilon = 1e-06


def layer_norm(values, gain_vec):
    average = jnp.mean(values, axis=-1, keepdims=True)
    centred = values - average
    variance = jnp.mean(centred * centred, axis=-1, keepdims=True)
    return centred * lax.rsqrt(variance + epsilon) * gain_vec


def on_device(
    clean_image,
    noise_draw,
    embed_weight,
    position_table,
    norm_gain,
    qkv_weight,
    query_gain,
    key_gain,
    out_weight,
):
    num_patches = position_table.shape[0]
    num_images = clean_image.shape[0] * lax.axis_size("mp")
    num_copies = noise_draw.shape[1] * lax.axis_size("dp")
    heads_here = qkv_weight.shape[2] // HEAD_DIM
    position_f = position_table.astype(jnp.float32)
    noisy_img = (
        clean_image[0].astype(jnp.float32) + 0.5 * noise_draw[0, 0].astype(jnp.float32)
    ).astype(jnp.bfloat16)
    all_pixels = lax.all_gather(noisy_img[None], "dp", axis=0, tiled=True)
    column_block = jnp.einsum(
        "ckp,kd->cpd", all_pixels, embed_weight, preferred_element_type=jnp.float32
    )
    moved = lax.all_to_all(
        column_block.astype(jnp.bfloat16), "dp", split_axis=0, concat_axis=2, tiled=True
    ).astype(column_block.dtype)
    owned = moved[0] + position_f
    normed_own = layer_norm(owned, norm_gain).astype(jnp.bfloat16)[:, None, :]
    projected = jnp.einsum(
        "pid,dtc->pitc",
        lax.all_gather(normed_own, "mp", axis=1, tiled=True),
        qkv_weight,
        preferred_element_type=jnp.float32,
    )
    query = projected[:, :, 0].reshape(num_patches, num_images, heads_here, HEAD_DIM)
    key_vec = projected[:, :, 1].reshape(num_patches, num_images, heads_here, HEAD_DIM)
    value = (
        projected[:, :, 2]
        .reshape(num_patches, num_images, heads_here, HEAD_DIM)
        .astype(jnp.bfloat16)
    )
    query = layer_norm(query, query_gain).astype(jnp.bfloat16)
    key_vec = layer_norm(key_vec, key_gain).astype(jnp.bfloat16)
    scores = jnp.einsum(
        "pihe,sihe->ihps", query, key_vec, preferred_element_type=jnp.float32
    ) * HEAD_DIM ** (-0.5)
    exp_scores = jnp.exp(scores)
    probs = (exp_scores / jnp.sum(exp_scores, axis=-1, keepdims=True)).astype(jnp.bfloat16)
    head_out = jnp.einsum("ihps,sihe->iphe", probs, value, preferred_element_type=jnp.float32)
    head_out = head_out.astype(jnp.bfloat16).reshape(num_images, num_patches, heads_here * HEAD_DIM)
    attention = lax.psum_scatter(
        jnp.einsum("ipc,cd->ipd", head_out, out_weight, preferred_element_type=jnp.float32).astype(
            jnp.bfloat16
        ),
        "mp",
        scatter_dimension=0,
        tiled=True,
    ).astype(jnp.float32)
    output = owned + attention[0]
    features = output.astype(jnp.bfloat16)[:, None, None, :]
    smoothed = lax.psum_scatter(
        (output[:, None, :] * (1.0 / num_copies)).astype(jnp.bfloat16),
        "dp",
        scatter_dimension=2,
        tiled=True,
    ).astype(jnp.float32)
    return (features, smoothed)


def solution(mesh):
    placed = (
        P("mp", None, None),
        P("mp", "dp", None, None),
        P(None, "dp"),
        P(),
        P(),
        P(None, None, "mp"),
        P(),
        P(),
        P("mp", None),
    )
    return jax.shard_map(
        on_device,
        mesh=mesh,
        in_specs=placed,
        out_specs=(P(None, "dp", "mp", None), P(None, "mp", "dp")),
        check_vma=False,
    )
```

profile of v0, /device:TPU:1, one launch (start us, length us, event | category | flops | bytes accessed | tf_op | source)
XLA Modules:
  0.0 414.4 jit_solution(16534508129750119568)
XLA Ops:
  7.2 1.8 fusion.19
  9.1 28.2 %all-gather.4.cloned.1.call-done = bf16[8,588,128]{2,1,0:T(8,128)(2,1)} async-done(((bf16[1,588,128]{2,1,0:T(8,128)(2,1)}), bf16[8,588,128]{2,1,0:T(8,128)(2,1)}) %all-gather.4.cloned.1.call-update) | async-done | bytes 1204240 | tf_op jit(solution)/shard_map/all_gather | solution.py:38
  37.2 2.7 convolution_convert_fusion
  39.9 22.4 %all_to_all.4 = bf16[8,128,768]{2,1,0:T(8,128)(2,1)S(1)} all-to-all(bf16[8,128,768]{2,1,0:T(8,128)(2,1)S(1)} %convolution_convert_fusion), channel_id=1, replica_groups=mesh['dp'=8,'mp'=4] {'dp'}, dimensions={0} | all-to-all | bytes 3145728 | tf_op jit(solution)/shard_map/all_to_all | solution.py:42
  62.4 2.0 convert_bitcast_fusion
  64.3 3.5 copy.29
  67.9 3.7 copy.30
  71.6 2.5 fusion.21
  74.1 0.3 copy-done.2
  74.4 0.6 multiply_reduce_fusion
  75.1 1.8 multiply_convert_fusion.1
  77.0 0.2 reduce-scatter.3.cloned.1.call-start
  77.2 115.2 %all-gather.6.cloned.1.call-done = bf16[128,24576]{1,0:T(8,128)(2,1)} async-done(((bf16[128,6144]{1,0:T(8,128)(2,1)}), bf16[128,24576]{1,0:T(8,128)(2,1)}) %all-gather.6.cloned.1.call-update) | async-done | bytes 6291472 | tf_op jit(solution)/shard_map/all_gather | solution.py:49
  192.4 8.6 %copy.31 = bf16[128,24576]{0,1:T(8,128)(2,1)} copy(bf16[128,24576]{1,0:T(8,128)(2,1)} %all-gather.6.cloned.1.call-done) | data formatting | bytes 12582912 | tf_op jit(solution)/shard_map/all_gather | solution.py:49
  201.0 20.5 %fusion = f32[128,4,3,768]{3,0,2,1:T(8,128)S(1)} fusion(bf16[128,4,6144,1]{0,2,3,1:T(8,128)(2,1)} %bitcast.52, bf16[6144,3,768]{2,0,1:T(8,128)(2,1)} %param.14), kind=kOutput, calls=%fused_computation | convolution fusion | flops 14495514624 | bytes 39321600 | tf_op jit(solution)/shard_map/pid,dtc->pitc/dot_general | solution.py:47
  221.5 0.1 slice.17
  221.6 1.9 fusion.22
  223.5 3.0 copy.35
  226.5 0.4 copy.33
  226.9 1.5 reduce_sum.67
  228.4 1.6 multiply_reduce_fusion.1
  230.0 3.0 copy.34
  233.1 1.5 reduce_sum.65
  234.6 1.7 multiply_reduce_fusion.2
  236.4 0.1 copy-done.4
  236.5 3.2 multiply_exponential_fusion
  239.7 2.4 convolution_convert_fusion.1
  242.1 10.7 %fusion.4 = bf16[4,128,6144]{2,1,0:T(8,128)(2,1)} fusion(bf16[4,128,768]{1,2,0:T(8,128)(2,1)S(1)} %bitcast.54, bf16[768,6144]{1,0:T(8,128)(2,1)} %param.17), kind=kOutput, calls=%fused_computation.4 | convolution fusion | flops 4834983936 | bytes 16515072 | tf_op jit(solution)/shard_map/ipc,cd->ipd/dot_general | solution.py:70
  252.9 108.9 %reduce-scatter.3.cloned.1.call-done = bf16[1,128,6144]{2,1,0:T(8,128)(2,1)} async-done(((bf16[4,128,6144]{2,1,0:T(8,128)(2,1)}), bf16[1,128,6144]{2,1,0:T(8,128)(2,1)}) %reduce-scatter.3.cloned.1.call-update) | async-done | bytes 1572880 | tf_op jit(solution)/shard_map/reduce_scatter | solution.py:69
  361.8 5.0 %fusion.9 = (bf16[128,1,6144]{2,0,1:T(8,128)(2,1)}, bf16[128,1,1,6144]{3,0,2,1:T(8,128)(2,1)}) fusion(bf16[1,128,6144]{2,1,0:T(8,128)(2,1)} %reduce-scatter.3.cloned.1.call-done, f32[128,6144]{1,0:T(8,128)} %copy.30, bf16[128,6144]{1,0:T(8,128)(2,1)S(1)} %copy-done.3), kind=kLoop, calls=%fused_computation.14 | loop fusion | flops 5505024 | bytes 9437184 | tf_op jit(solution)/shard_map/convert_element_type | solution.py:80
  366.8 39.1 %reduce-scatter.5.cloned.1.call-done = bf16[128,1,768]{2,0,1:T(8,128)(2,1)} async-done(((bf16[128,1,6144]{2,0,1:T(8,128)(2,1)}), bf16[128,1,768]{2,0,1:T(8,128)(2,1)}) %reduce-scatter.5.cloned.1.call-update) | async-done | bytes 196624 | tf_op jit(solution)/shard_map/reduce_scatter | solution.py:79
  405.9 2.0 copy.40
  (26 shorter events, 0.3 us)
Async XLA Ops:
  7.2 30.1 %copy-start = (bf16[588,768]{1,0:T(8,128)(2,1)S(1)}, bf16[588,768]{1,0:T(8,128)(2,1)}, u32[]{:S(2)}) copy-start(bf16[588,768]{1,0:T(8,128)(2,1)} %param.11) | copy-start | bytes 2709508
  7.2 30.0 %all-gather.4.cloned.1.call-start = ((), (), s32[]{:S(2)}) async-start(), calls=%async_computation.3 | async-start | bytes 1363968 | tf_op jit(solution)/shard_map/all_gather | solution.py:38
  9.0 183.4 %all-gather.6.cloned.1.call-start = ((), (), s32[]{:S(2)}) async-start(), calls=%async_computation.6 | async-start | bytes 7864320 | tf_op jit(solution)/shard_map/all_gather | solution.py:49
  67.9 3.7 copy-start.3
  71.6 2.8 copy-start.2
  74.4 0.7 copy-start.5
  77.0 284.8 %reduce-scatter.3.cloned.1.call-start = ((), (), s32[]{:S(2)}) async-start(), calls=%async_computation.4 | async-start | bytes 7864320 | tf_op jit(solution)/shard_map/reduce_scatter | solution.py:69
  233.1 3.3 copy-start.6
  233.1 3.3 copy-start.7
  234.6 1.9 copy-start.4
  252.8 153.0 %reduce-scatter.5.cloned.1.call-start = ((), (), s32[]{:S(2)}) async-start(), calls=%async_computation.5 | async-start | bytes 1769472 | tf_op jit(solution)/shard_map/reduce_scatter | solution.py:79
  361.8 46.1 %copy-start.1 = (bf16[588,768]{1,0:T(8,128)(2,1)S(1)}, bf16[588,768]{1,0:T(8,128)(2,1)}, u32[]{:S(2)}) copy-start(bf16[588,768]{1,0:T(8,128)(2,1)} %param.11) | copy-start | bytes 2709508
Sparse Core Ops, SparseCore 0:
  10.5 26.7 all-gather.3
  77.1 115.3 all-gather.5
  252.9 108.7 reduce-scatter.2
  366.9 38.9 reduce-scatter.4
where the time goes:
time: 416 us; the launch traced here: 414 us
  waiting for transfers between devices  291 us (70%)
  matrix products  39.5 us (9%)
  local copies, waits for them, and re-layouts  26.7 us (6%)
  blocking collectives  22.4 us (5%)
  other arithmetic  20.1 us (5%)
  between operations  13.9 us (3%)
    all_gather x1, waiting for transfers between devices, on_device(): lax.all_gather(normed_own, 'mp', axis=1, tiled=True)  115 us
    reduce_scatter x1, waiting for transfers between devices, on_device(): lax.psum_scatter(jnp.einsum('ipc,cd->ipd', head_out, out_weight, preferre...  109 us
    reduce_scatter x1, waiting for transfers between devices, on_device(): lax.psum_scatter((output[:, None, :] * (1.0 / num_copies)).astype(jnp.bfl...  39.1 us
    all_gather x1, waiting for transfers between devices, on_device(): all_pixels = lax.all_gather(noisy_img[None], 'dp', axis=0, tiled=True)  28.2 us
    all_to_all x1, blocking collectives, on_device(): lax.all_to_all(column_block.astype(jnp.bfloat16), 'dp', split_axis=0, con...  22.4 us
    dot_general x1, matrix products, on_device(): jnp.einsum('pid,dtc->pitc', lax.all_gather(normed_own, 'mp', axis=1, tile...  20.5 us
    dot_general x1, matrix products, on_device(): jnp.einsum('ipc,cd->ipd', head_out, out_weight, preferred_element_type=jn...  10.7 us
    all_gather x1, local copies, waits for them, and re-layouts, on_device(): lax.all_gather(normed_own, 'mp', axis=1, tiled=True)  8.62 us
  transfers between devices with their start and end apart: 4, of which 4 were waited for; matrix products, arithmetic and copies ran while one was open for 0% of the time, Pallas kernels for 0%

commit v1 on v0

v1 whole, which is shorter than its diff:
```python
import functools

import jax
import jax.numpy as jnp
from jax import lax
from jax.experimental import pallas as pl
from jax.experimental.pallas import tpu as pltpu
from jax.sharding import PartitionSpec as P

HEAD_DIM = 128
MESH = pl.DeviceIdType.MESH
EPSILON = 1e-06


def round_up(value, step):
    return (value + step - 1) // step * step


def remote(src, dst, send_sem, recv_sem, axis, target):
    return pltpu.make_async_remote_copy(
        src_ref=src,
        dst_ref=dst,
        send_sem=send_sem,
        recv_sem=recv_sem,
        device_id={axis: target},
        device_id_type=MESH,
    )


def greet(sizes):
    barrier = pltpu.get_barrier_semaphore()
    total = 0
    for axis, size in sizes:
        me = lax.axis_index(axis)
        for step in range(1, size):
            pl.semaphore_signal(
                barrier,
                inc=1,
                device_id={axis: lax.rem(me + step, size)},
                device_id_type=MESH,
            )
        total += size - 1
    pl.semaphore_wait(barrier, total)


class Gather:
    def __init__(self, size, own, slot, halves, send_sem, recv_sem, half_sem):
        self.size = size
        self.me = lax.axis_index("dp")
        self.core = lax.rem(self.me, 2)
        self.chip = self.me // 2
        self.chips = size // 2
        self.own, self.slot, self.halves = own, slot, halves
        self.send_sem, self.recv_sem, self.half_sem = send_sem, recv_sem, half_sem
        self.sent = []
        self.relay = self.chips == 4
        self.sibling = self.chip * 2 + 1 - self.core
        if self.relay:
            x = self.chip + 1 - 2 * lax.rem(self.chip, 2)
            y = lax.rem(self.chip + 2, 4)
            d = lax.rem(x + 2, 4)
            self.order = [x, y, d]
        else:
            self.order = [lax.rem(self.chip + j, self.chips) for j in range(1, self.chips)]

    def push(self, src, dst, recv, target):
        copy = remote(src, dst, self.send_sem.at[len(self.sent)], recv, "dp", target)
        copy.start()
        self.sent.append(copy)

    def start(self):
        me = self.me
        for chip in self.order[: 2 if self.relay else None]:
            self.push(self.own, self.slot(me), self.recv_sem.at[me], chip * 2 + self.core)
        self.push(self.own, self.slot(me), self.recv_sem.at[me], self.sibling)

    def wait_slot(self, source):
        there = self.slot(source)
        remote(there, there, self.send_sem.at[0], self.recv_sem.at[source], "dp", self.sibling).wait_recv()

    def to_sibling(self, source):
        there = self.slot(source)
        self.push(there, there, self.recv_sem.at[source], self.sibling)

    def arrive(self, step):
        source = self.order[step] * 2 + self.core
        if self.relay and step == 2:
            for half in range(2):
                part = self.halves(source, half)
                remote(part, part, self.send_sem.at[0], self.half_sem.at[half], "dp", self.sibling).wait_recv()
        else:
            self.wait_slot(source)
            if self.relay:
                part = self.halves(source, step)
                other = self.order[1 - step] * 2 + self.core
                self.push(part, part, self.half_sem.at[step], other)
        self.to_sibling(source)
        return source

    def arrive_sibling(self, step):
        source = self.order[step] * 2 + 1 - self.core
        self.wait_slot(source)
        return source

    def finish(self):
        for copy in self.sent:
            copy.wait_send()


def sends(size):
    chips = size // 2
    return (chips - 1) + 1 + (chips - 1) + 2


def heads_kernel(
    nd, nm, noisy_ref, embed_ref, position_ref, gain_ref, qkv_ref, qgain_ref, kgain_ref, out_ref,
    pixels, blocks, embedded, normed, weights, projected, outgoing, arrived,
    z_send, z_recv, w_send, w_recv, w_half, h_send, h_recv, load_sem,
):
    here = lax.axis_index("mp")
    patches = position_ref.shape[0]
    width = embed_ref.shape[1]
    rows, rows_full = embed_ref.shape[0], blocks.shape[1]
    total = nm * patches
    pairs, chunk = outgoing.shape[0], outgoing.shape[3]
    heads = chunk // HEAD_DIM

    def load(kind, pair):
        return pltpu.make_async_copy(
            qkv_ref.at[kind, :, pl.ds(pl.multiple_of(pair * chunk, HEAD_DIM), chunk)],
            weights.at[kind],
            load_sem.at[kind],
        )

    for kind in range(3):
        load(kind, 0).start()
    if rows_full > rows:
        blocks[:, rows:, :] = jnp.zeros((nd, rows_full - rows, width), blocks.dtype)
    greet((("dp", nd), ("mp", nm)))

    gather = Gather(
        nd,
        embed_ref,
        lambda s: blocks.at[s, pl.ds(0, rows)],
        lambda s, half: blocks.at[s, pl.ds(0, rows), pl.ds(half * (width // 2), width // 2)],
        w_send, w_recv, w_half,
    )
    pixel_copies = []
    for step in range(1, nm):
        copy = remote(
            noisy_ref, pixels.at[here], z_send.at[step - 1], z_recv.at[here], "mp",
            lax.rem(here + step, nm),
        )
        copy.start()
        pixel_copies.append(copy)
    gather.start()
    pixels[here] = noisy_ref[...]
    blocks[gather.me, :rows, :] = embed_ref[...]
    for step in range(1, nm):
        source = lax.rem(here + step, nm)
        remote(
            noisy_ref, pixels.at[source], z_send.at[0], z_recv.at[source], "mp", source
        ).wait_recv()

    part = 256 if width % 256 == 0 else 128

    def embed(source):
        @pl.loop(0, width // part)
        def _(n):
            cols = pl.ds(pl.multiple_of(n * part, part), part)
            product = jnp.dot(
                pixels[...].reshape(total, rows_full),
                blocks[source, :, cols],
                preferred_element_type=jnp.float32,
            )
            place = position_ref[:, pl.ds(pl.multiple_of(source * width + n * part, part), part)]
            product = product.reshape(nm, patches, part) + place.astype(jnp.float32)[None]
            embedded[source, :, cols] = product.reshape(total, part)

    embed(gather.me)
    steps = len(gather.order)
    gather.wait_slot(gather.sibling)
    embed(gather.sibling)
    if gather.relay:
        near = [gather.arrive(0), gather.arrive(1)]
        for source in near:
            embed(source)
        for step in range(2):
            embed(gather.arrive_sibling(step))
        embed(gather.arrive(2))
        embed(gather.arrive_sibling(2))
    else:
        for step in range(steps):
            embed(gather.arrive(step))
        for step in range(steps):
            embed(gather.arrive_sibling(step))

    band = 16
    features = nd * width

    @pl.loop(0, total // band)
    def _(r):
        at = pl.ds(pl.multiple_of(r * band, band), band)
        values = embedded[:, at, :]
        mean = jnp.sum(jnp.sum(values, axis=0), axis=-1, keepdims=True) * (1.0 / features)
        centred = embedded[:, at, :] - mean[None]
        square = jnp.sum(jnp.sum(centred * centred, axis=0), axis=-1, keepdims=True)
        scale = lax.rsqrt(square * (1.0 / features) + EPSILON)
        normed[:, at, :] = (
            (embedded[:, at, :] - mean[None]) * scale[None] * gain_ref[...]
        ).astype(normed.dtype)

    def head_norm(values, gain):
        mean = jnp.mean(values, axis=-1, keepdims=True)
        centred = values - mean
        variance = jnp.mean(centred * centred, axis=-1, keepdims=True)
        return (centred * lax.rsqrt(variance + EPSILON) * gain[...]).astype(jnp.bfloat16)

    def exchange(pair, step):
        target = lax.rem(here + step, nm)
        return remote(
            outgoing.at[pair, target], arrived.at[here, pair],
            h_send.at[pair, step - 1], h_recv.at[pair, here], "mp", target,
        )

    @pl.loop(0, pairs)
    def _(pair):
        for kind in range(3):
            load(kind, pair).wait()
            for s in range(nd):
                product = jnp.dot(
                    normed[s], weights[kind, s * width : (s + 1) * width, :],
                    preferred_element_type=jnp.float32,
                )
                if s == 0:
                    projected[kind] = product
                else:
                    projected[kind] += product

            @pl.when(pair + 1 < pairs)
            def _():
                load(kind, pair + 1).start()

        @pl.loop(0, nm)
        def _(image):
            at = pl.ds(pl.multiple_of(image * patches, patches), patches)
            for head in range(heads):
                cols = slice(head * HEAD_DIM, (head + 1) * HEAD_DIM)
                query = head_norm(projected[0, at, cols], qgain_ref)
                key = head_norm(projected[1, at, cols], kgain_ref)
                value = projected[2, at, cols].astype(jnp.bfloat16)
                scores = lax.dot_general(
                    query, key, (((1,), (1,)), ((), ())), preferred_element_type=jnp.float32
                ) * HEAD_DIM ** (-0.5)
                powers = jnp.exp(scores)
                probs = (powers / jnp.sum(powers, axis=-1, keepdims=True)).astype(jnp.bfloat16)
                result = jnp.dot(probs, value, preferred_element_type=jnp.float32)
                outgoing[pair, image, :, cols] = result.astype(jnp.bfloat16)

        for step in range(1, nm):
            exchange(pair, step).start()
        arrived[here, pair] = outgoing[pair, here]

    for copy in pixel_copies:
        copy.wait_send()
    gather.finish()
    for pair in range(pairs):
        for step in range(1, nm):
            exchange(pair, step).wait_send()
            source = lax.rem(here + step, nm)
            remote(
                outgoing.at[pair, source], arrived.at[source, pair],
                h_send.at[pair, step - 1], h_recv.at[pair, source], "mp", source,
            ).wait_recv()
    out_ref[...] = arrived[...]


def output_kernel(
    nd, heads_ref, noisy_ref, embed_ref, position_ref, out_weight_ref, features_ref, smoothed_ref,
    held, residual, outgoing, incoming, g_send, g_recv, g_half, f_send, f_recv,
):
    me = lax.axis_index("dp")
    nm, pairs, patches, chunk = heads_ref.shape
    width = embed_ref.shape[1]
    rows = embed_ref.shape[0]
    greet((("dp", nd),))
    gather = Gather(
        nd,
        heads_ref,
        lambda s: held.at[s],
        lambda s, half: held.at[s, pl.ds(half * (nm // 2), nm // 2)],
        g_send, g_recv, g_half,
    )
    gather.start()
    held[me] = heads_ref[...]
    place = position_ref[...].astype(jnp.float32)

    @pl.loop(0, nd)
    def _(c):
        residual[c] = (
            jnp.dot(noisy_ref[c], embed_ref[...], preferred_element_type=jnp.float32) + place
        )

    smoothed_ref[...] = jnp.zeros_like(smoothed_ref)
    part = 256 if width % 256 == 0 else 128
    both = 2 * patches

    def give(copy):
        return remote(
            outgoing.at[copy], incoming.at[me], f_send.at[copy], f_recv.at[me], "dp", copy
        )

    def project(chip):
        first = chip * 2

        @pl.loop(0, width // part)
        def _(n):
            cols = pl.ds(pl.multiple_of(n * part, part), part)
            left = jnp.concatenate(
                [
                    held[pl.ds(first, 2), h, p].reshape(both, chunk)
                    for h in range(nm)
                    for p in range(pairs)
                ],
                axis=1,
            )
            product = jnp.dot(left, out_weight_ref[:, cols], preferred_element_type=jnp.float32)
            result = residual[pl.ds(first, 2), :, cols] + product.reshape(2, patches, part)
            outgoing[pl.ds(first, 2), :, cols] = result.astype(outgoing.dtype)
            smoothed_ref[:, cols] += jnp.sum(result, axis=0) * (1.0 / nd)

    gather.wait_slot(gather.sibling)
    steps = len(gather.order)
    project(gather.chip)
    give(gather.sibling).start()
    incoming[me] = outgoing[me]

    def finish_chip(step):
        gather.arrive_sibling(step)
        chip = gather.order[step]
        project(chip)
        for core in range(2):
            give(chip * 2 + core).start()

    if gather.relay:
        gather.arrive(0)
        gather.arrive(1)
        finish_chip(0)
        finish_chip(1)
        gather.arrive(2)
        finish_chip(2)
    else:
        for step in range(steps):
            gather.arrive(step)
        for step in range(steps):
            finish_chip(step)
    gather.finish()

    features_ref[:, pl.ds(pl.multiple_of(me * width, HEAD_DIM), width)] = incoming[me]
    for step in range(1, nd):
        source = lax.rem(me + step, nd)
        give(source).wait_send()
        remote(
            outgoing.at[source], incoming.at[source], f_send.at[source], f_recv.at[source],
            "dp", source,
        ).wait_recv()
        features_ref[:, pl.ds(pl.multiple_of(source * width, HEAD_DIM), width)] = incoming[source]


VMEM = pl.BlockSpec(memory_space=pltpu.VMEM)
DMA = pltpu.SemaphoreType.DMA


def on_device(
    clean_image, noise_draw, embed_weight, position_table, norm_gain, qkv_weight,
    query_gain, key_gain, out_weight,
):
    nd, nm = lax.axis_size("dp"), lax.axis_size("mp")
    patches, features = position_table.shape
    pixels, width = embed_weight.shape
    group = qkv_weight.shape[2]
    heads = group // HEAD_DIM
    chunk = HEAD_DIM * (2 if heads % 2 == 0 else 1)
    pairs = group // chunk
    rows, rows_full = round_up(pixels, 16), round_up(pixels, 128)
    me = lax.axis_index("dp")

    own_columns = lax.dynamic_slice_in_dim(out_weight, me * width, width, axis=1)
    out_columns = lax.all_gather(own_columns, "mp", axis=0, tiled=True)
    noisy = (
        clean_image[0].astype(jnp.float32) + 0.5 * noise_draw[0, 0].astype(jnp.float32)
    ).astype(jnp.bfloat16)
    noisy = jnp.pad(noisy.T, ((0, 0), (0, rows_full - pixels)))
    embed_padded = jnp.pad(embed_weight, ((0, rows - pixels), (0, 0)))
    noisy_copies = lax.all_gather(noisy[None], "dp", axis=0, tiled=True)

    bf16, f32 = jnp.bfloat16, jnp.float32
    total = nm * patches
    head_out = pl.pallas_call(
        functools.partial(heads_kernel, nd, nm),
        out_shape=jax.ShapeDtypeStruct((nm, pairs, patches, chunk), bf16),
        in_specs=[VMEM] * 4 + [pl.BlockSpec(memory_space=pl.ANY)] + [VMEM] * 2,
        out_specs=VMEM,
        scratch_shapes=[
            pltpu.VMEM((nm, patches, rows_full), bf16),
            pltpu.VMEM((nd, rows_full, width), bf16),
            pltpu.VMEM((nd, total, width), f32),
            pltpu.VMEM((nd, total, width), bf16),
            pltpu.VMEM((3, features, chunk), bf16),
            pltpu.VMEM((3, total, chunk), f32),
            pltpu.VMEM((pairs, nm, patches, chunk), bf16),
            pltpu.VMEM((nm, pairs, patches, chunk), bf16),
            DMA((nm,)), DMA((nm,)),
            DMA((sends(nd),)), DMA((nd,)), DMA((2,)),
            DMA((pairs, nm)), DMA((pairs, nm)),
            DMA((3,)),
        ],
        compiler_params=pltpu.CompilerParams(
            collective_id=0, has_side_effects=True, vmem_limit_bytes=60 * 1024 * 1024
        ),
        cost_estimate=pl.CostEstimate(
            flops=2 * total * features * 4 * group, bytes_accessed=qkv_weight.size * 2,
            transcendentals=0,
        ),
        name="embed_and_heads",
    )(
        noisy,
        embed_padded,
        position_table,
        norm_gain.reshape(nd, 1, width),
        jnp.transpose(qkv_weight, (1, 0, 2)),
        query_gain.reshape(1, HEAD_DIM),
        key_gain.reshape(1, HEAD_DIM),
    )

    own_position = lax.dynamic_slice_in_dim(position_table, me * width, width, axis=1)
    embed_full = jnp.pad(embed_weight, ((0, rows_full - pixels), (0, 0)))
    features_out, smoothed = pl.pallas_call(
        functools.partial(output_kernel, nd),
        out_shape=(
            jax.ShapeDtypeStruct((patches, features), bf16),
            jax.ShapeDtypeStruct((patches, width), f32),
        ),
        in_specs=[VMEM] * 5,
        out_specs=(VMEM, VMEM),
        scratch_shapes=[
            pltpu.VMEM((nd, nm, pairs, patches, chunk), bf16),
            pltpu.VMEM((nd, patches, width), f32),
            pltpu.VMEM((nd, patches, width), bf16),
            pltpu.VMEM((nd, patches, width), bf16),
            DMA((sends(nd),)), DMA((nd,)), DMA((2,)),
            DMA((nd,)), DMA((nd,)),
        ],
        compiler_params=pltpu.CompilerParams(
            collective_id=1, has_side_effects=True, vmem_limit_bytes=48 * 1024 * 1024
        ),
        cost_estimate=pl.CostEstimate(
            flops=2 * nd * patches * nm * group * width, bytes_accessed=2 * nm * group * width,
            transcendentals=0,
        ),
        name="project_and_share",
    )(head_out, noisy_copies, embed_full, own_position, out_columns)
    return features_out[:, None, None, :], smoothed[:, None, :]


def solution(mesh):
    placed = (
        P("mp", None, None),
        P("mp", "dp", None, None),
        P(None, "dp"),
        P(),
        P(),
        P(None, None, "mp"),
        P(),
        P(),
        P("mp", None),
    )
    return jax.shard_map(
        on_device,
        mesh=mesh,
        in_specs=placed,
        out_specs=(P(None, "dp", "mp", None), P(None, "mp", "dp")),
        check_vma=False,
    )
```

time: 416 us -> 214 us (0.51)
  waiting for transfers between devices: 291 us -> 30.7 us
  Pallas kernels: 0 us -> 156 us
  matrix products: 39.5 us -> 0 us
  blocking collectives: 22.4 us -> 0 us
  other arithmetic: 20.1 us -> 0.05 us
  local copies, waits for them, and re-layouts: 26.7 us -> 12 us
    pallas_call x0 -> x2, Pallas kernels: none -> 156 us  [the longest x1 106 us: on_device(): pl.pallas_call(functools.partial(heads_kernel, nd, nm), out_shape=jax.Sha...]
    reduce_scatter x2 -> x0, waiting for transfers between devices: 148 us -> none  [the longest x1 109 us: on_device(): lax.psum_scatter(jnp.einsum('ipc,cd->ipd', head_out, out_weight, preferre...]
    all_gather x2, waiting for transfers between devices: 143 us -> 30.7 us  [the longest x1 30.7 us: on_device(): out_columns = lax.all_gather(own_columns, 'mp', axis=0, tiled=True)]
    dot_general x5 -> x0, matrix products: 39.5 us -> none  [the longest x1 20.5 us: on_device(): jnp.einsum('pid,dtc->pitc', lax.all_gather(normed_own, 'mp', axis=1, tile...]
    all_to_all x1 -> x0, blocking collectives: 22.4 us -> none  [on_device(): lax.all_to_all(column_block.astype(jnp.bfloat16), 'dp', split_axis=0, con...]
    convert_element_type x4 -> x0, other arithmetic: 10.5 us -> none  [the longest x1 4.97 us: on_device(): (output[:, None, :] * (1.0 / num_copies)).astype(jnp.bfloat16)]
    reduce_sum x6 -> x0, other arithmetic: 9.52 us -> none  [the longest x3 5.56 us: layer_norm(): average = jnp.mean(values, axis=-1, keepdims=True)]
    all_gather x1 -> x0, local copies, waits for them, and re-layouts: 8.62 us -> none  [on_device(): lax.all_gather(normed_own, 'mp', axis=1, tiled=True)]
  transfers between devices with their start and end apart: 4 -> 2, of which waited for: 4 -> 1; matrix products, arithmetic and copies ran while one was open for 0% -> 2% of each run, Pallas kernels for 0% -> 50%
where the time goes in v1:
time: 214 us; the launch traced here: 213 us
  Pallas kernels  156 us (73%)
  waiting for transfers between devices  30.7 us (14%)
  between operations  14.1 us (7%)
  local copies, waits for them, and re-layouts  12 us (6%)
    pallas_call x1, Pallas kernels, on_device(): pl.pallas_call(functools.partial(heads_kernel, nd, nm), out_shape=jax.Sha...  106 us
    pallas_call x1, Pallas kernels, on_device(): pl.pallas_call(functools.partial(output_kernel, nd), out_shape=(jax.Shape...  50.7 us
    all_gather x1, waiting for transfers between devices, on_device(): out_columns = lax.all_gather(own_columns, 'mp', axis=0, tiled=True)  30.7 us
    unnamed x10, local copies, waits for them, and re-layouts  6.88 us
  transfers between devices with their start and end apart: 2, of which 1 were waited for; matrix products, arithmetic and copies ran while one was open for 2% of the time, Pallas kernels for 50%

profile of v1, /device:TPU:1, one launch (start us, length us, event | category | flops | bytes accessed | tf_op | source)
XLA Modules:
  0.0 213.2 jit_solution(9654203656544575332)
XLA Ops:
  7.2 0.0 all-gather.6.cloned.1.call-start
  7.2 1.1 copy.11
  8.3 1.1 copy.12
  9.3 0.1 fusion.1
  9.4 0.7 pad.12.noisy_ref
  10.1 0.0 all-gather.6.cloned.1.call-update
  10.1 0.0 all-gather.4.cloned.1.call-start
  10.2 0.0 copy-start.2
  10.2 2.4 %constant_dynamic-slice_fusion = bf16[768,768]{1,0:T(8,128)(2,1)} fusion(bf16[768,6144]{1,0:T(8,128)(2,1)} %param.17, s32[]{:T(128)S(6)} %select_n.4), kind=kLoop, calls=%fused_computation.3 | loop fusion | bytes 2359300 | tf_op jit(solution)/shard_map/dynamic_slice | solution.py:388
  12.6 0.0 all-gather.4.cloned.1.call-update
  12.6 0.0 copy-done.2
  12.7 1.0 pad.13.embed_ref
  13.6 0.1 pad.14.embed_ref
  13.7 0.9 constant_dynamic-slice_fusion.1.position_ref
  14.7 105.6 %embed_and_heads.1.heads_ref = bf16[4,3,128,256]{3,2,1,0:T(8,128)(2,1)} custom-call(bf16[128,640]{1,0:T(8,128)(2,1)} %pad.12.noisy_ref, bf16[592,768]{1,0:T(8,128)(2,1)} %pad.13.embed_ref, bf16[128,6144]{1,0:T(8,128)(2,1)} %position_ref.1, f32[8,1,768]{2,1,0:T(1,128)} %bitcast.20, bf16[3,6144,768]{2,1,0:T(8,128)(2,1)} %bitcast.19, f32[1,128]{1,0:T(1,128)} %bitcast.21, ...), custom_call_target="tpu_custom_call" | custom-call | flops 19327352832 | bytes 28311552 | tf_op jit(solution)/shard_map/embed_and_heads/pallas_call | solution.py:399
  120.3 0.0 all-gather.6.cloned.1.call-done
  120.3 30.7 %all-gather.4.cloned.1.call-done.out_weight_ref = bf16[3072,768]{1,0:T(8,128)(2,1)} async-done(((bf16[768,768]{1,0:T(8,128)(2,1)}), bf16[3072,768]{1,0:T(8,128)(2,1)}) %all-gather.4.cloned.1.call-update) | async-done | bytes 4718608 | tf_op jit(solution)/shard_map/all_gather | solution.py:389
  151.0 0.0 copy-start
  151.0 1.3 copy-done
  152.3 0.0 copy-start.1
  152.3 1.1 copy-done.1
  153.4 50.7 %project_and_share.1 = (bf16[128,6144]{1,0:T(8,128)(2,1)S(1)}, f32[128,768]{1,0:T(8,128)S(1)}) custom-call(bf16[4,3,128,256]{3,2,1,0:T(8,128)(2,1)S(1)} %copy-done.1, bf16[8,128,640]{2,1,0:T(8,128)(2,1)S(1)} %bitcast.18, bf16[640,768]{1,0:T(8,128)(2,1)S(1)} %pad.14.embed_ref, bf16[128,768]{1,0:T(8,128)(2,1)S(1)} %constant_dynamic-slice_fusion.1.position_ref, ...), custom_call_target="tpu_custom_call" | custom-call | flops 4831838208 | bytes 4718592 | tf_op jit(solution)/shard_map/project_and_share/pallas_call | solution.py:438
  204.1 1.2 copy.13
  205.3 1.1 copy.15
Async XLA Ops:
  7.2 113.1 %all-gather.6.cloned.1.call-start = ((), (), s32[]{:S(2)}) async-start(), calls=%async_computation.1 | async-start | bytes 1474560 | tf_op jit(solution)/shard_map/all_gather | solution.py:395
  10.1 140.9 %all-gather.4.cloned.1.call-start = ((), (), s32[]{:S(2)}) async-start(), calls=%async_computation | async-start | bytes 5898240 | tf_op jit(solution)/shard_map/all_gather | solution.py:389
  10.2 2.5 %copy-start.2 = (bf16[588,768]{1,0:T(8,128)(2,1)S(1)}, bf16[588,768]{1,0:T(8,128)(2,1)}, u32[]{:S(2)}) copy-start(bf16[588,768]{1,0:T(8,128)(2,1)} %param.11) | copy-start | bytes 2709508
  151.0 1.3 copy-start
  152.3 1.1 copy-start.1
Sparse Core Ops, SparseCore 0:
  10.5 32.6 all-gather.5
  45.2 105.6 all-gather.3

commit v2 on v1

--- a/solution.py
+++ b/solution.py
@@ -112,32 +112,89 @@
     return (chips - 1) + 1 + (chips - 1) + 2
 
 
+class Line:
+    def __init__(self, size, own, slot, send_sem, recv_sem):
+        self.size = size
+        self.here = lax.axis_index("mp")
+        self.own, self.slot = own, slot
+        self.send_sem, self.recv_sem = send_sem, recv_sem
+
+    def ways(self, hop):
+        for side, step in enumerate((1, -1)):
+            source = self.here - step * hop
+            target = self.here + step
+            held = (source >= 0) & (source < self.size)
+            yield side, source, target, held, held & (target >= 0) & (target < self.size)
+
+    def copy(self, hop, side, source, target):
+        src = self.own if hop == 0 else self.slot(source)
+        return remote(
+            src, self.slot(source), self.send_sem.at[hop, side], self.recv_sem.at[source], "mp", target
+        )
+
+    def hop(self, hop):
+        for side, source, target, held, onward in self.ways(hop):
+            if hop > 0:
+                @pl.when(held)
+                def _():
+                    self.copy(hop, side, source, target).wait_recv()
+
+            if hop < self.size - 1:
+                @pl.when(onward)
+                def _():
+                    self.copy(hop, side, source, target).start()
+
+    def finish(self):
+        for hop in range(self.size - 1):
+            for side, source, target, _, onward in self.ways(hop):
+                @pl.when(onward)
+                def _():
+                    self.copy(hop, side, source, target).wait_send()
+
+
 def heads_kernel(
-    nd, nm, noisy_ref, embed_ref, position_ref, gain_ref, qkv_ref, qgain_ref, kgain_ref, out_ref,
-    pixels, blocks, embedded, normed, weights, projected, outgoing, arrived,
-    z_send, z_recv, w_send, w_recv, w_half, h_send, h_recv, load_sem,
+    nd, nm, clean_ref, noise_ref, embed_ref, position_ref, gain_ref, qgain_ref, kgain_ref,
+    qkv_ref, out_weight_ref, held_ref, columns_ref, copies_ref,
+    raised, pixels, blocks, embedded, means, squares, normed, weights, projected, outgoing,
+    z_send, z_recv, w_send, w_recv, w_half, h_send, h_recv, g_send, g_recv, g_half,
+    o_send, o_recv, c_send, c_recv, load_sem, own_sem,
 ):
+    me = lax.axis_index("dp")
     here = lax.axis_index("mp")
     patches = position_ref.shape[0]
     width = embed_ref.shape[1]
     rows, rows_full = embed_ref.shape[0], blocks.shape[1]
+    count = clean_ref.shape[0]
     total = nm * patches
+    features = nd * width
     pairs, chunk = outgoing.shape[0], outgoing.shape[3]
     heads = chunk // HEAD_DIM
 
     def load(kind, pair):
         return pltpu.make_async_copy(
-            qkv_ref.at[kind, :, pl.ds(pl.multiple_of(pair * chunk, HEAD_DIM), chunk)],
-            weights.at[kind],
-            load_sem.at[kind],
+            qkv_ref.at[kind, :, pl.ds(pair * chunk, chunk)], weights.at[kind], load_sem.at[kind]
         )
 
     for kind in range(3):
         load(kind, 0).start()
+    own_columns = out_weight_ref.at[:, pl.ds(pl.multiple_of(me * width, HEAD_DIM), width)]
+    keep = [pltpu.make_async_copy(own_columns, columns_ref.at[here], own_sem.at[0])]
+    keep[0].start()
+    raised[...] = jnp.zeros_like(raised)
+    raised[:count, :] = clean_ref[...].astype(jnp.float32) + 0.5 * noise_ref[...].astype(jnp.float32)
+    pixels[here] = raised[...].T.astype(pixels.dtype)
     if rows_full > rows:
         blocks[:, rows:, :] = jnp.zeros((nd, rows_full - rows, width), blocks.dtype)
     greet((("dp", nd), ("mp", nm)))
 
+    def pixel_copy(step):
+        target = lax.rem(here + step, nm)
+        return remote(
+            pixels.at[here], pixels.at[here], z_send.at[step - 1], z_recv.at[here], "mp", target
+        )
+
+    for step in range(1, nm):
+        pixel_copy(step).start()
     gather = Gather(
         nd,
         embed_ref,
@@ -145,26 +202,25 @@
         lambda s, half: blocks.at[s, pl.ds(0, rows), pl.ds(half * (width // 2), width // 2)],
         w_send, w_recv, w_half,
     )
-    pixel_copies = []
-    for step in range(1, nm):
-        copy = remote(
-            noisy_ref, pixels.at[here], z_send.at[step - 1], z_recv.at[here], "mp",
-            lax.rem(here + step, nm),
-        )
-        copy.start()
-        pixel_copies.append(copy)
     gather.start()
-    pixels[here] = noisy_ref[...]
-    blocks[gather.me, :rows, :] = embed_ref[...]
+    line = Line(nm, own_columns, lambda s: columns_ref.at[s], o_send, o_recv)
+    line.hop(0)
+    blocks[me, :rows, :] = embed_ref[...]
     for step in range(1, nm):
         source = lax.rem(here + step, nm)
         remote(
-            noisy_ref, pixels.at[source], z_send.at[0], z_recv.at[source], "mp", source
+            pixels.at[here], pixels.at[source], z_send.at[0], z_recv.at[source], "mp", source
         ).wait_recv()
 
     part = 256 if width % 256 == 0 else 128
+    band = 64
+
+    done = []
 
     def embed(source):
+        before = len(done)
+        done.append(source)
+
         @pl.loop(0, width // part)
         def _(n):
             cols = pl.ds(pl.multiple_of(n * part, part), part)
@@ -177,7 +233,22 @@
             product = product.reshape(nm, patches, part) + place.astype(jnp.float32)[None]
             embedded[source, :, cols] = product.reshape(total, part)
 
-    embed(gather.me)
+        @pl.loop(0, total // band)
+        def _(r):
+            at = pl.ds(pl.multiple_of(r * band, band), band)
+            values = embedded[source, at, :]
+            mean = jnp.mean(values, axis=-1, keepdims=True)
+            centred = values - mean
+            square = jnp.sum(centred * centred, axis=-1, keepdims=True)
+            if before == 0:
+                means[at, :] = mean
+                squares[at, :] = square
+            else:
+                apart = mean - means[at, :]
+                means[at, :] += apart * (1.0 / (before + 1))
+                squares[at, :] += square + apart * apart * (width * before / (before + 1))
+
+    embed(me)
     steps = len(gather.order)
     gather.wait_slot(gather.sibling)
     embed(gather.sibling)
@@ -187,28 +258,38 @@
             embed(source)
         for step in range(2):
             embed(gather.arrive_sibling(step))
-        embed(gather.arrive(2))
+        far = gather.arrive(2)
+        line.hop(1)
+        embed(far)
         embed(gather.arrive_sibling(2))
     else:
         for step in range(steps):
             embed(gather.arrive(step))
+        if nm > 1:
+            line.hop(1)
         for step in range(steps):
             embed(gather.arrive_sibling(step))
 
-    band = 16
-    features = nd * width
+    def copy_pixels(step):
+        return remote(
+            pixels.at[here], copies_ref.at[me], c_send.at[step - 1], c_recv.at[me], "dp",
+            lax.rem(me + step, nd),
+        )
+
+    for step in range(1, nd):
+        copy_pixels(step).start()
+    keep.append(pltpu.make_async_copy(pixels.at[here], copies_ref.at[me], own_sem.at[1]))
+    keep[1].start()
 
     @pl.loop(0, total // band)
     def _(r):
         at = pl.ds(pl.multiple_of(r * band, band), band)
-        values = embedded[:, at, :]
-        mean = jnp.sum(jnp.sum(values, axis=0), axis=-1, keepdims=True) * (1.0 / features)
-        centred = embedded[:, at, :] - mean[None]
-        square = jnp.sum(jnp.sum(centred * centred, axis=0), axis=-1, keepdims=True)
-        scale = lax.rsqrt(square * (1.0 / features) + EPSILON)
-        normed[:, at, :] = (
-            (embedded[:, at, :] - mean[None]) * scale[None] * gain_ref[...]
-        ).astype(normed.dtype)
+        mean = means[at, :]
+        scale = lax.rsqrt(squares[at, :] * (1.0 / features) + EPSILON)
+        for s in range(nd):
+            normed[at, s * width : (s + 1) * width] = (
+                (embedded[s, at, :] - mean) * scale * gain_ref[s]
+            ).astype(normed.dtype)
 
     def head_norm(values, gain):
         mean = jnp.mean(values, axis=-1, keepdims=True)
@@ -219,31 +300,60 @@
     def exchange(pair, step):
         target = lax.rem(here + step, nm)
         return remote(
-            outgoing.at[pair, target], arrived.at[here, pair],
+            outgoing.at[pair, target], held_ref.at[me, pair, here],
             h_send.at[pair, step - 1], h_recv.at[pair, here], "mp", target,
         )
 
-    @pl.loop(0, pairs)
-    def _(pair):
+    def keep_heads(pair):
+        return pltpu.make_async_copy(
+            outgoing.at[pair, here], held_ref.at[me, pair, here], own_sem.at[2 + pair]
+        )
+
+    shares = []
+
+    def share(pair):
+        keep_heads(pair).wait()
+        for step in range(1, nm):
+            source = lax.rem(here + step, nm)
+            remote(
+                outgoing.at[pair, source], held_ref.at[me, pair, source],
+                h_send.at[pair, step - 1], h_recv.at[pair, source], "mp", source,
+            ).wait_recv()
+        shares.append(
+            Gather(
+                nd,
+                held_ref.at[me, pair],
+                lambda s: held_ref.at[s, pair],
+                lambda s, half: held_ref.at[s, pair, pl.ds(half * (nm // 2), nm // 2)],
+                g_send.at[pair], g_recv.at[pair], g_half.at[pair],
+            )
+        )
+        shares[pair].start()
+
+    def pass_near(pair):
+        for step in range(min(2, steps)):
+            shares[pair].arrive(step)
+
+    def pass_far(pair):
+        for step in range(2, steps):
+            shares[pair].arrive(step)
+
+    for pair in range(pairs):
         for kind in range(3):
             load(kind, pair).wait()
-            for s in range(nd):
-                product = jnp.dot(
-                    normed[s], weights[kind, s * width : (s + 1) * width, :],
-                    preferred_element_type=jnp.float32,
-                )
-                if s == 0:
-                    projected[kind] = product
-                else:
-                    projected[kind] += product
-
-            @pl.when(pair + 1 < pairs)
-            def _():
+            projected[kind] = jnp.dot(
+                normed[...], weights[kind], preferred_element_type=jnp.float32
+            )
+            if pair + 1 < pairs:
                 load(kind, pair + 1).start()
-
-        @pl.loop(0, nm)
-        def _(image):
-            at = pl.ds(pl.multiple_of(image * patches, patches), patches)
+            if kind == 1:
+                if pair >= 2:
+                    pass_far(pair - 2)
+                if pair >= 1:
+                    share(pair - 1)
+
+        for image in range(nm):
+            at = slice(image * patches, (image + 1) * patches)
             for head in range(heads):
                 cols = slice(head * HEAD_DIM, (head + 1) * HEAD_DIM)
                 query = head_norm(projected[0, at, cols], qgain_ref)
@@ -259,48 +369,52 @@
 
         for step in range(1, nm):
             exchange(pair, step).start()
-        arrived[here, pair] = outgoing[pair, here]
-
-    for copy in pixel_copies:
-        copy.wait_send()
+        keep_heads(pair).start()
+        if pair == 0 and nm > 2:
+            line.hop(2)
+        if pair >= 1:
+            pass_near(pair - 1)
+
+    last = pairs - 1
+    share(last)
+    if last >= 1:
+        pass_far(last - 1)
+    pass_near(last)
+    pass_far(last)
+
+    for copy in keep:
+        copy.wait()
+    for hop in range(3, nm + 1):
+        line.hop(hop)
+    line.finish()
+    for step in range(1, nm):
+        pixel_copy(step).wait_send()
+    for step in range(1, nd):
+        copy_pixels(step).wait_send()
+        source = lax.rem(me + step, nd)
+        remote(
+            pixels.at[here], copies_ref.at[source], c_send.at[0], c_recv.at[source], "dp", source
+        ).wait_recv()
     gather.finish()
     for pair in range(pairs):
         for step in range(1, nm):
             exchange(pair, step).wait_send()
-            source = lax.rem(here + step, nm)
-            remote(
-                outgoing.at[pair, source], arrived.at[source, pair],
-                h_send.at[pair, step - 1], h_recv.at[pair, source], "mp", source,
-            ).wait_recv()
-    out_ref[...] = arrived[...]
+        for step in range(steps):
+            shares[pair].arrive_sibling(step)
+        shares[pair].wait_slot(shares[pair].sibling)
+        shares[pair].finish()
 
 
 def output_kernel(
     nd, heads_ref, noisy_ref, embed_ref, position_ref, out_weight_ref, features_ref, smoothed_ref,
-    held, residual, outgoing, incoming, g_send, g_recv, g_half, f_send, f_recv,
+    outgoing, incoming, f_send, f_recv,
 ):
     me = lax.axis_index("dp")
-    nm, pairs, patches, chunk = heads_ref.shape
+    _, pairs, nm, patches, chunk = heads_ref.shape
     width = embed_ref.shape[1]
-    rows = embed_ref.shape[0]
+    rows, rows_full = embed_ref.shape[0], noisy_ref.shape[2]
     greet((("dp", nd),))
-    gather = Gather(
-        nd,
-        heads_ref,
-        lambda s: held.at[s],
-        lambda s, half: held.at[s, pl.ds(half * (nm // 2), nm // 2)],
-        g_send, g_recv, g_half,
-    )
-    gather.start()
-    held[me] = heads_ref[...]
-    place = position_ref[...].astype(jnp.float32)
-
-    @pl.loop(0, nd)
-    def _(c):
-        residual[c] = (
-            jnp.dot(noisy_ref[c], embed_ref[...], preferred_element_type=jnp.float32) + place
-        )
-
+    start = pl.ds(pl.multiple_of(me * width, HEAD_DIM), width)
     smoothed_ref[...] = jnp.zeros_like(smoothed_ref)
     part = 256 if width % 256 == 0 else 128
     both = 2 * patches
@@ -318,45 +432,33 @@
             cols = pl.ds(pl.multiple_of(n * part, part), part)
             left = jnp.concatenate(
                 [
-                    held[pl.ds(first, 2), h, p].reshape(both, chunk)
+                    heads_ref[pl.ds(first, 2), p, h].reshape(both, chunk)
                     for h in range(nm)
                     for p in range(pairs)
                 ],
                 axis=1,
             )
-            product = jnp.dot(left, out_weight_ref[:, cols], preferred_element_type=jnp.float32)
-            result = residual[pl.ds(first, 2), :, cols] + product.reshape(2, patches, part)
+            product = jnp.dot(
+                left, out_weight_ref[:, cols], preferred_element_type=jnp.float32
+            )
+            noisy = noisy_ref[pl.ds(first, 2)].reshape(both, rows_full)[:, :rows]
+            base = jnp.dot(noisy, embed_ref[:, cols], preferred_element_type=jnp.float32)
+            place = position_ref[:, pl.ds(pl.multiple_of(me * width + n * part, part), part)]
+            result = (product + base).reshape(2, patches, part) + place.astype(jnp.float32)[None]
             outgoing[pl.ds(first, 2), :, cols] = result.astype(outgoing.dtype)
             smoothed_ref[:, cols] += jnp.sum(result, axis=0) * (1.0 / nd)
 
-    gather.wait_slot(gather.sibling)
-    steps = len(gather.order)
-    project(gather.chip)
-    give(gather.sibling).start()
-    incoming[me] = outgoing[me]
-
-    def finish_chip(step):
-        gather.arrive_sibling(step)
-        chip = gather.order[step]
+    here = me // 2
+    chips = nd // 2
+    for step in range(1, chips):
+        chip = lax.rem(here + step, chips)
         project(chip)
         for core in range(2):
             give(chip * 2 + core).start()
-
-    if gather.relay:
-        gather.arrive(0)
-        gather.arrive(1)
-        finish_chip(0)
-        finish_chip(1)
-        gather.arrive(2)
-        finish_chip(2)
-    else:
-        for step in range(steps):
-            gather.arrive(step)
-        for step in range(steps):
-            finish_chip(step)
-    gather.finish()
-
-    features_ref[:, pl.ds(pl.multiple_of(me * width, HEAD_DIM), width)] = incoming[me]
+    project(here)
+    sibling = here * 2 + 1 - lax.rem(me, 2)
+    give(sibling).start()
+    features_ref[:, start] = outgoing[me]
     for step in range(1, nd):
         source = lax.rem(me + step, nd)
         give(source).wait_send()
@@ -383,40 +485,42 @@
     chunk = HEAD_DIM * (2 if heads % 2 == 0 else 1)
     pairs = group // chunk
     rows, rows_full = round_up(pixels, 16), round_up(pixels, 128)
-    me = lax.axis_index("dp")
-
-    own_columns = lax.dynamic_slice_in_dim(out_weight, me * width, width, axis=1)
-    out_columns = lax.all_gather(own_columns, "mp", axis=0, tiled=True)
-    noisy = (
-        clean_image[0].astype(jnp.float32) + 0.5 * noise_draw[0, 0].astype(jnp.float32)
-    ).astype(jnp.bfloat16)
-    noisy = jnp.pad(noisy.T, ((0, 0), (0, rows_full - pixels)))
+
     embed_padded = jnp.pad(embed_weight, ((0, rows - pixels), (0, 0)))
-    noisy_copies = lax.all_gather(noisy[None], "dp", axis=0, tiled=True)
 
     bf16, f32 = jnp.bfloat16, jnp.float32
     total = nm * patches
-    head_out = pl.pallas_call(
+    anywhere = pl.BlockSpec(memory_space=pl.ANY)
+    held, columns, copies = pl.pallas_call(
         functools.partial(heads_kernel, nd, nm),
-        out_shape=jax.ShapeDtypeStruct((nm, pairs, patches, chunk), bf16),
-        in_specs=[VMEM] * 4 + [pl.BlockSpec(memory_space=pl.ANY)] + [VMEM] * 2,
-        out_specs=VMEM,
+        out_shape=(
+            jax.ShapeDtypeStruct((nd, pairs, nm, patches, chunk), bf16),
+            jax.ShapeDtypeStruct((nm, group, width), bf16),
+            jax.ShapeDtypeStruct((nd, patches, rows_full), bf16),
+        ),
+        in_specs=[VMEM] * 7 + [anywhere] * 2,
+        out_specs=(anywhere,) * 3,
         scratch_shapes=[
+            pltpu.VMEM((rows_full, patches), f32),
             pltpu.VMEM((nm, patches, rows_full), bf16),
             pltpu.VMEM((nd, rows_full, width), bf16),
             pltpu.VMEM((nd, total, width), f32),
-            pltpu.VMEM((nd, total, width), bf16),
+            pltpu.VMEM((total, 1), f32),
+            pltpu.VMEM((total, 1), f32),
+            pltpu.VMEM((total, features), bf16),
             pltpu.VMEM((3, features, chunk), bf16),
             pltpu.VMEM((3, total, chunk), f32),
             pltpu.VMEM((pairs, nm, patches, chunk), bf16),
-            pltpu.VMEM((nm, pairs, patches, chunk), bf16),
             DMA((nm,)), DMA((nm,)),
             DMA((sends(nd),)), DMA((nd,)), DMA((2,)),
             DMA((pairs, nm)), DMA((pairs, nm)),
-            DMA((3,)),
+            DMA((pairs, sends(nd))), DMA((pairs, nd)), DMA((pairs, 2)),
+            DMA((nm, 2)), DMA((nm,)),
+            DMA((nd,)), DMA((nd,)),
+            DMA((3,)), DMA((2 + pairs,)),
         ],
         compiler_params=pltpu.CompilerParams(
-            collective_id=0, has_side_effects=True, vmem_limit_bytes=60 * 1024 * 1024
+            collective_id=0, has_side_effects=True, vmem_limit_bytes=62 * 1024 * 1024
         ),
         cost_estimate=pl.CostEstimate(
             flops=2 * total * features * 4 * group, bytes_accessed=qkv_weight.size * 2,
@@ -424,17 +528,17 @@
         ),
         name="embed_and_heads",
     )(
-        noisy,
+        clean_image[0],
+        noise_draw[0, 0],
         embed_padded,
         position_table,
         norm_gain.reshape(nd, 1, width),
-        jnp.transpose(qkv_weight, (1, 0, 2)),
         query_gain.reshape(1, HEAD_DIM),
         key_gain.reshape(1, HEAD_DIM),
+        jnp.transpose(qkv_weight, (1, 0, 2)),
+        out_weight,
     )
 
-    own_position = lax.dynamic_slice_in_dim(position_table, me * width, width, axis=1)
-    embed_full = jnp.pad(embed_weight, ((0, rows_full - pixels), (0, 0)))
     features_out, smoothed = pl.pallas_call(
         functools.partial(output_kernel, nd),
         out_shape=(
@@ -444,11 +548,8 @@
         in_specs=[VMEM] * 5,
         out_specs=(VMEM, VMEM),
         scratch_shapes=[
-            pltpu.VMEM((nd, nm, pairs, patches, chunk), bf16),
-            pltpu.VMEM((nd, patches, width), f32),
             pltpu.VMEM((nd, patches, width), bf16),
             pltpu.VMEM((nd, patches, width), bf16),
-            DMA((sends(nd),)), DMA((nd,)), DMA((2,)),
             DMA((nd,)), DMA((nd,)),
         ],
         compiler_params=pltpu.CompilerParams(
@@ -459,7 +560,7 @@
             transcendentals=0,
         ),
         name="project_and_share",
-    )(head_out, noisy_copies, embed_full, own_position, out_columns)
+    )(held, copies, embed_padded, position_table, columns.reshape(nm * group, width))
     return features_out[:, None, None, :], smoothed[:, None, :]
 
 

time: 214 us -> 170 us (0.79)
  waiting for transfers between devices: 30.7 us -> 0 us
  between operations: 14.1 us -> 0.66 us
  Pallas kernels: 156 us -> 161 us
  local copies, waits for them, and re-layouts: 12 us -> 7.17 us
    all_gather x2 -> x0, waiting for transfers between devices: 30.7 us -> none  [the longest x1 30.7 us: on_device(): out_columns = lax.all_gather(own_columns, 'mp', axis=0, tiled=True)]
    pallas_call x1, Pallas kernels: 106 us -> 135 us  [on_device(): pl.pallas_call(functools.partial(heads_kernel, nd, nm), out_shape=(jax.Sh...]
    pallas_call x1, Pallas kernels: 50.7 us -> 26.6 us  [on_device(): pl.pallas_call(functools.partial(output_kernel, nd), out_shape=(jax.Shape...]
    dynamic_slice x2 -> x0, local copies, waits for them, and re-layouts: 3.39 us -> none  [the longest x1 2.44 us: on_device(): lax.dynamic_slice_in_dim(out_weight, me * width, width, axis=1)]
    unnamed x10 -> x8, local copies, waits for them, and re-layouts: 6.88 us -> 5.02 us
  transfers between devices with their start and end apart: 2 -> 0, of which waited for: 1 -> 0; matrix products, arithmetic and copies ran while one was open for 2% -> 0% of each run, Pallas kernels for 50% -> 0%
where the time goes in v2:
time: 170 us; the launch traced here: 169 us
  Pallas kernels  161 us (95%)
  local copies, waits for them, and re-layouts  7.17 us (4%)
    pallas_call x1, Pallas kernels, on_device(): pl.pallas_call(functools.partial(heads_kernel, nd, nm), out_shape=(jax.Sh...  135 us
    pallas_call x1, Pallas kernels, on_device(): pl.pallas_call(functools.partial(output_kernel, nd), out_shape=(jax.Shape...  26.6 us
    unnamed x8, local copies, waits for them, and re-layouts  5.02 us

profile of v2, /device:TPU:1, one launch (start us, length us, event | category | flops | bytes accessed | tf_op | source)
XLA Modules:
  0.0 169.3 jit_solution(14791442962984965012)
XLA Ops:
  0.6 2.2 %pad.4.embed_ref = bf16[592,768]{1,0:T(8,128)(2,1)} pad(bf16[588,768]{1,0:T(8,128)(2,1)} %param.11, bf16[]{:T(256)} %constant.2.clone.1), padding=0_4x0_0 | pad | bytes 1812482 | tf_op jit(solution)/shard_map/jit(_pad)/pad | solution.py:489
  2.8 0.0 copy-start
  2.8 134.9 %embed_and_heads.1 = (bf16[8,3,4,128,256]{4,3,2,1,0:T(8,128)(2,1)}, bf16[4,768,768]{2,1,0:T(8,128)(2,1)}, bf16[8,128,640]{2,1,0:T(8,128)(2,1)}) custom-call(bf16[588,128]{1,0:T(8,128)(2,1)} %bitcast.12, bf16[588,128]{1,0:T(8,128)(2,1)} %bitcast.13, bf16[592,768]{1,0:T(8,128)(2,1)} %pad.4.embed_ref, bf16[128,6144]{1,0:T(8,128)(2,1)} %position_ref.3, ...), custom_call_target="tpu_custom_call" | custom-call | flops 19327352832 | bytes 28311552 | tf_op jit(solution)/shard_map/embed_and_heads/pallas_call | solution.py:494
  137.7 0.0 copy-done
  137.7 0.0 copy-start.1
  137.7 1.4 copy-done.1
  139.1 0.0 copy-start.2
  139.1 1.3 copy-done.2
  140.4 26.6 %project_and_share.1 = (bf16[128,6144]{1,0:T(8,128)(2,1)S(1)}, f32[128,768]{1,0:T(8,128)S(1)}) custom-call(bf16[8,3,4,128,256]{4,3,2,1,0:T(8,128)(2,1)} %get-tuple-element.7.heads_ref, bf16[8,128,640]{2,1,0:T(8,128)(2,1)S(1)} %copy-done.2, bf16[592,768]{1,0:T(8,128)(2,1)S(1)} %copy-done, bf16[128,6144]{1,0:T(8,128)(2,1)S(1)} %copy-done.1, ...), custom_call_target="tpu_custom_call" | custom-call | flops 4831838208 | bytes 4718592 | tf_op jit(solution)/shard_map/project_and_share/pallas_call | solution.py:542
  167.0 1.2 copy.11
  168.2 1.1 copy.13
Async XLA Ops:
  2.8 134.9 %copy-start = (bf16[592,768]{1,0:T(8,128)(2,1)S(1)}, bf16[592,768]{1,0:T(8,128)(2,1)}, u32[]{:S(2)}) copy-start(bf16[592,768]{1,0:T(8,128)(2,1)} %pad.4.embed_ref) | copy-start | bytes 2727940
  137.7 1.4 copy-start.1
  139.1 1.3 copy-start.2

commit v3 on v2

--- a/solution.py
+++ b/solution.py
@@ -112,10 +112,19 @@
     return (chips - 1) + 1 + (chips - 1) + 2
 
 
+def late_panel(size):
+    return size > 2
+
+
+def panel_width(width):
+    return 256 if width % 256 == 0 else 128
+
+
 class Line:
-    def __init__(self, size, own, slot, send_sem, recv_sem):
+    def __init__(self, size, own, slot, early, send_sem, recv_sem):
         self.size = size
         self.here = lax.axis_index("mp")
+        self.early = early
         self.own, self.slot = own, slot
         self.send_sem, self.recv_sem = send_sem, recv_sem
 
@@ -127,9 +136,11 @@
             yield side, source, target, held, held & (target >= 0) & (target < self.size)
 
     def copy(self, hop, side, source, target):
-        src = self.own if hop == 0 else self.slot(source)
+        src, dst = self.own if hop == 0 else self.slot(source), self.slot(source)
+        if late_panel(self.size) and hop == self.size - 2:
+            src, dst = src.at[:, self.early], dst.at[:, self.early]
         return remote(
-            src, self.slot(source), self.send_sem.at[hop, side], self.recv_sem.at[source], "mp", target
+            src, dst, self.send_sem.at[hop, side], self.recv_sem.at[source], "mp", target
         )
 
     def hop(self, hop):
@@ -137,7 +148,7 @@
             if hop > 0:
                 @pl.when(held)
                 def _():
-                    self.copy(hop, side, source, target).wait_recv()
+                    self.copy(hop - 1, side, source, target).wait_recv()
 
             if hop < self.size - 1:
                 @pl.when(onward)
@@ -163,8 +174,9 @@
     here = lax.axis_index("mp")
     patches = position_ref.shape[0]
     width = embed_ref.shape[1]
-    rows, rows_full = embed_ref.shape[0], blocks.shape[1]
-    count = clean_ref.shape[0]
+    count, rows_full = clean_ref.shape[0], blocks.shape[1]
+    rows = round_up(count, 16)
+    tail = count // 16 * 16
     total = nm * patches
     features = nd * width
     pairs, chunk = outgoing.shape[0], outgoing.shape[3]
@@ -183,8 +195,9 @@
     raised[...] = jnp.zeros_like(raised)
     raised[:count, :] = clean_ref[...].astype(jnp.float32) + 0.5 * noise_ref[...].astype(jnp.float32)
     pixels[here] = raised[...].T.astype(pixels.dtype)
-    if rows_full > rows:
-        blocks[:, rows:, :] = jnp.zeros((nd, rows_full - rows, width), blocks.dtype)
+    if rows_full > tail:
+        blocks[:, tail:, :] = jnp.zeros((nd, rows_full - tail, width), blocks.dtype)
+    blocks[me, :count, :] = embed_ref[...]
     greet((("dp", nd), ("mp", nm)))
 
     def pixel_copy(step):
@@ -197,22 +210,22 @@
         pixel_copy(step).start()
     gather = Gather(
         nd,
-        embed_ref,
+        blocks.at[me, pl.ds(0, rows)],
         lambda s: blocks.at[s, pl.ds(0, rows)],
         lambda s, half: blocks.at[s, pl.ds(0, rows), pl.ds(half * (width // 2), width // 2)],
         w_send, w_recv, w_half,
     )
     gather.start()
-    line = Line(nm, own_columns, lambda s: columns_ref.at[s], o_send, o_recv)
+    part = panel_width(width)
+    early = pl.ds(0, width - part)
+    line = Line(nm, own_columns, lambda s: columns_ref.at[s], early, o_send, o_recv)
     line.hop(0)
-    blocks[me, :rows, :] = embed_ref[...]
     for step in range(1, nm):
         source = lax.rem(here + step, nm)
         remote(
             pixels.at[here], pixels.at[source], z_send.at[0], z_recv.at[source], "mp", source
         ).wait_recv()
 
-    part = 256 if width % 256 == 0 else 128
     band = 64
 
     done = []
@@ -259,8 +272,8 @@
         for step in range(2):
             embed(gather.arrive_sibling(step))
         far = gather.arrive(2)
+        embed(far)
         line.hop(1)
-        embed(far)
         embed(gather.arrive_sibling(2))
     else:
         for step in range(steps):
@@ -347,6 +360,9 @@
             if pair + 1 < pairs:
                 load(kind, pair + 1).start()
             if kind == 1:
+                if pair == min(1, pairs - 1):
+                    for hop in range(2, min(3, nm)):
+                        line.hop(hop)
                 if pair >= 2:
                     pass_far(pair - 2)
                 if pair >= 1:
@@ -370,8 +386,6 @@
         for step in range(1, nm):
             exchange(pair, step).start()
         keep_heads(pair).start()
-        if pair == 0 and nm > 2:
-            line.hop(2)
         if pair >= 1:
             pass_near(pair - 1)
 
@@ -406,67 +420,134 @@
 
 
 def output_kernel(
-    nd, heads_ref, noisy_ref, embed_ref, position_ref, out_weight_ref, features_ref, smoothed_ref,
-    outgoing, incoming, f_send, f_recv,
+    nd, nm, heads_ref, noisy_ref, embed_ref, position_ref, columns_ref, features_ref, smoothed_ref,
+    weights, embed_full, outgoing, incoming, f_send, f_recv, late_send, late_recv, load_sem,
 ):
     me = lax.axis_index("dp")
-    _, pairs, nm, patches, chunk = heads_ref.shape
+    here = lax.axis_index("mp")
+    _, pairs, _, patches, chunk = heads_ref.shape
     width = embed_ref.shape[1]
-    rows, rows_full = embed_ref.shape[0], noisy_ref.shape[2]
-    greet((("dp", nd),))
-    start = pl.ds(pl.multiple_of(me * width, HEAD_DIM), width)
+    count, rows_full = embed_ref.shape[0], noisy_ref.shape[2]
+    group = columns_ref.shape[1]
+    part = panel_width(width)
+    panels = width // part
+    early, late = pl.ds(0, width - part), pl.ds(width - part, part)
+    both = 2 * patches
+
+    first_load = pltpu.make_async_copy(
+        columns_ref.at[:, :, early], weights.at[:, :, early], load_sem.at[nm]
+    )
+    first_load.start()
+
+    def late_loads():
+        for source in range(nm):
+            near = (here - source < nm - 1) & (source - here < nm - 1)
+            copy = pltpu.make_async_copy(
+                columns_ref.at[source, :, late], weights.at[source, :, late], load_sem.at[source]
+            )
+            yield near if late_panel(nm) else here >= 0, copy
+
+    for near, copy in late_loads():
+        @pl.when(near)
+        def _():
+            copy.start()
+
+    greet((("dp", nd), ("mp", nm)))
+
+    def late_hop(side, step, source, target):
+        return remote(
+            columns_ref.at[source, :, late], weights.at[source, :, late],
+            late_send.at[side], late_recv.at[side], "mp", target,
+        )
+
+    def late_sends():
+        for side, step in enumerate((1, -1)):
+            source, target = here - step * (nm - 2), here + step
+            go = (source >= 0) & (source < nm) & (target >= 0) & (target < nm)
+            yield go, late_hop(side, step, source, target)
+
+    if late_panel(nm):
+        for go, copy in late_sends():
+            @pl.when(go)
+            def _():
+                copy.start()
+
+    embed_full[count // 16 * 16 :, :] = jnp.zeros(
+        (rows_full - count // 16 * 16, width), embed_full.dtype
+    )
+    embed_full[:count, :] = embed_ref[...]
     smoothed_ref[...] = jnp.zeros_like(smoothed_ref)
-    part = 256 if width % 256 == 0 else 128
-    both = 2 * patches
-
-    def give(copy):
+
+    def give(panel, copy):
         return remote(
-            outgoing.at[copy], incoming.at[me], f_send.at[copy], f_recv.at[me], "dp", copy
-        )
-
-    def project(chip):
-        first = chip * 2
-
-        @pl.loop(0, width // part)
-        def _(n):
-            cols = pl.ds(pl.multiple_of(n * part, part), part)
-            left = jnp.concatenate(
-                [
-                    heads_ref[pl.ds(first, 2), p, h].reshape(both, chunk)
-                    for h in range(nm)
-                    for p in range(pairs)
-                ],
-                axis=1,
-            )
-            product = jnp.dot(
-                left, out_weight_ref[:, cols], preferred_element_type=jnp.float32
-            )
-            noisy = noisy_ref[pl.ds(first, 2)].reshape(both, rows_full)[:, :rows]
-            base = jnp.dot(noisy, embed_ref[:, cols], preferred_element_type=jnp.float32)
-            place = position_ref[:, pl.ds(pl.multiple_of(me * width + n * part, part), part)]
-            result = (product + base).reshape(2, patches, part) + place.astype(jnp.float32)[None]
-            outgoing[pl.ds(first, 2), :, cols] = result.astype(outgoing.dtype)
-            smoothed_ref[:, cols] += jnp.sum(result, axis=0) * (1.0 / nd)
-
-    here = me // 2
+            outgoing.at[panel, copy], incoming.at[panel, me],
+            f_send.at[panel, copy], f_recv.at[panel, me], "dp", copy,
+        )
+
+    def project(panel, chip):
+        pair = pl.ds(chip * 2, 2)
+        cols = slice(panel * part, (panel + 1) * part)
+        left = jnp.concatenate(
+            [heads_ref[pair, p, h].reshape(both, chunk) for h in range(nm) for p in range(pairs)],
+            axis=1,
+        )
+        product = jnp.dot(
+            left, weights[:, :, cols].reshape(nm * group, part), preferred_element_type=jnp.float32
+        )
+        base = jnp.dot(
+            noisy_ref[pair].reshape(both, rows_full), embed_full[:, cols],
+            preferred_element_type=jnp.float32,
+        )
+        place = position_ref[:, pl.ds(pl.multiple_of(me * width + panel * part, part), part)]
+        result = (product + base).reshape(2, patches, part) + place.astype(jnp.float32)[None]
+        outgoing[panel, pair] = result.astype(outgoing.dtype)
+        smoothed_ref[:, cols] += jnp.sum(result, axis=0) * (1.0 / nd)
+
+    chip_here = me // 2
     chips = nd // 2
-    for step in range(1, chips):
-        chip = lax.rem(here + step, chips)
-        project(chip)
-        for core in range(2):
-            give(chip * 2 + core).start()
-    project(here)
-    sibling = here * 2 + 1 - lax.rem(me, 2)
-    give(sibling).start()
-    features_ref[:, start] = outgoing[me]
-    for step in range(1, nd):
-        source = lax.rem(me + step, nd)
-        give(source).wait_send()
-        remote(
-            outgoing.at[source], incoming.at[source], f_send.at[source], f_recv.at[source],
-            "dp", source,
-        ).wait_recv()
-        features_ref[:, pl.ds(pl.multiple_of(source * width, HEAD_DIM), width)] = incoming[source]
+    sibling = chip_here * 2 + 1 - lax.rem(me, 2)
+    first_load.wait()
+    for panel in range(panels):
+        if panel == panels - 1:
+            for near, copy in late_loads():
+                @pl.when(near)
+                def _():
+                    copy.wait()
+
+            if late_panel(nm):
+                for side, step in enumerate((1, -1)):
+                    source = here - step * (nm - 1)
+
+                    @pl.when((source >= 0) & (source < nm))
+                    def _():
+                        late_hop(side, step, source, here - step).wait_recv()
+
+        for step in range(1, chips):
+            chip = lax.rem(chip_here + step, chips)
+            project(panel, chip)
+            for core in range(2):
+                give(panel, chip * 2 + core).start()
+        project(panel, chip_here)
+        give(panel, sibling).start()
+        at = pl.ds(pl.multiple_of(me * width + panel * part, part), part)
+        features_ref[:, at] = outgoing[panel, me]
+
+    if late_panel(nm):
+        for go, copy in late_sends():
+            @pl.when(go)
+            def _():
+                copy.wait_send()
+
+    for panel in range(panels):
+        for step in range(1, nd):
+            source = lax.rem(me + step, nd)
+            give(panel, source).wait_send()
+            remote(
+                outgoing.at[panel, source], incoming.at[panel, source],
+                f_send.at[panel, source], f_recv.at[panel, source], "dp", source,
+            ).wait_recv()
+            at = pl.ds(pl.multiple_of(source * width + panel * part, part), part)
+            features_ref[:, at] = incoming[panel, source]
 
 
 VMEM = pl.BlockSpec(memory_space=pltpu.VMEM)
@@ -484,9 +565,9 @@
     heads = group // HEAD_DIM
     chunk = HEAD_DIM * (2 if heads % 2 == 0 else 1)
     pairs = group // chunk
-    rows, rows_full = round_up(pixels, 16), round_up(pixels, 128)
-
-    embed_padded = jnp.pad(embed_weight, ((0, rows - pixels), (0, 0)))
+    rows_full = round_up(pixels, 128)
+
+    part = panel_width(width)
 
     bf16, f32 = jnp.bfloat16, jnp.float32
     total = nm * patches
@@ -530,7 +611,7 @@
     )(
         clean_image[0],
         noise_draw[0, 0],
-        embed_padded,
+        embed_weight,
         position_table,
         norm_gain.reshape(nd, 1, width),
         query_gain.reshape(1, HEAD_DIM),
@@ -540,17 +621,20 @@
     )
 
     features_out, smoothed = pl.pallas_call(
-        functools.partial(output_kernel, nd),
+        functools.partial(output_kernel, nd, nm),
         out_shape=(
             jax.ShapeDtypeStruct((patches, features), bf16),
             jax.ShapeDtypeStruct((patches, width), f32),
         ),
-        in_specs=[VMEM] * 5,
+        in_specs=[VMEM] * 4 + [anywhere],
         out_specs=(VMEM, VMEM),
         scratch_shapes=[
-            pltpu.VMEM((nd, patches, width), bf16),
-            pltpu.VMEM((nd, patches, width), bf16),
-            DMA((nd,)), DMA((nd,)),
+            pltpu.VMEM((nm, group, width), bf16),
+            pltpu.VMEM((rows_full, width), bf16),
+            pltpu.VMEM((width // part, nd, patches, part), bf16),
+            pltpu.VMEM((width // part, nd, patches, part), bf16),
+            DMA((width // part, nd)), DMA((width // part, nd)),
+            DMA((2,)), DMA((2,)), DMA((nm + 1,)),
         ],
         compiler_params=pltpu.CompilerParams(
             collective_id=1, has_side_effects=True, vmem_limit_bytes=48 * 1024 * 1024
@@ -560,7 +644,7 @@
             transcendentals=0,
         ),
         name="project_and_share",
-    )(held, copies, embed_padded, position_table, columns.reshape(nm * group, width))
+    )(held, copies, embed_weight, position_table, columns)
     return features_out[:, None, None, :], smoothed[:, None, :]
 
 

time: 170 us -> 159 us (0.935)
  Pallas kernels: 161 us -> 153 us
  local copies, waits for them, and re-layouts: 7.17 us -> 4.78 us
    pallas_call x1, Pallas kernels: 135 us -> 127 us  [on_device(): pl.pallas_call(functools.partial(heads_kernel, nd, nm), out_shape=(jax.Sh...]
    pad x1 -> x0, local copies, waits for them, and re-layouts: 2.16 us -> none  [on_device(): embed_padded = jnp.pad(embed_weight, ((0, rows - pixels), (0, 0)))]
where the time goes in v3:
time: 159 us
  Pallas kernels  153 us (96%)
  local copies, waits for them, and re-layouts  4.78 us (3%)
    pallas_call x1, Pallas kernels, on_device(): pl.pallas_call(functools.partial(heads_kernel, nd, nm), out_shape=(jax.Sh...  127 us
    pallas_call x1, Pallas kernels, on_device(): pl.pallas_call(functools.partial(output_kernel, nd, nm), out_shape=(jax.S...  26.8 us
    unnamed x8, local copies, waits for them, and re-layouts  4.78 us

profile of v3, /device:TPU:1, one launch (start us, length us, event | category | flops | bytes accessed | tf_op | source)
XLA Modules:
  0.0 158.9 jit_solution(3089837400310185267)
XLA Ops:
  0.6 0.0 copy-start
  0.6 126.6 %embed_and_heads.1 = (bf16[8,3,4,128,256]{4,3,2,1,0:T(8,128)(2,1)}, bf16[4,768,768]{2,1,0:T(8,128)(2,1)}, bf16[8,128,640]{2,1,0:T(8,128)(2,1)}) custom-call(bf16[588,128]{1,0:T(8,128)(2,1)} %bitcast.11, bf16[588,128]{1,0:T(8,128)(2,1)} %bitcast.12, bf16[588,768]{1,0:T(8,128)(2,1)} %embed_ref.3, bf16[128,6144]{1,0:T(8,128)(2,1)} %position_ref.3, ...), custom_call_target="tpu_custom_call" | custom-call | flops 19327352832 | bytes 28311552 | tf_op jit(solution)/shard_map/embed_and_heads/pallas_call | solution.py:575
  127.2 0.0 copy-done
  127.2 0.0 copy-start.1
  127.2 1.2 copy-done.1
  128.4 0.0 copy-start.2
  128.4 1.3 copy-done.2
  129.7 26.8 %project_and_share.1 = (bf16[128,6144]{1,0:T(8,128)(2,1)S(1)}, f32[128,768]{1,0:T(8,128)S(1)}) custom-call(bf16[8,3,4,128,256]{4,3,2,1,0:T(8,128)(2,1)} %get-tuple-element.7.heads_ref, bf16[8,128,640]{2,1,0:T(8,128)(2,1)S(1)} %copy-done.2, bf16[588,768]{1,0:T(8,128)(2,1)S(1)} %copy-done.1, bf16[128,6144]{1,0:T(8,128)(2,1)S(1)} %copy-done, ...), custom_call_target="tpu_custom_call" | custom-call | flops 4831838208 | bytes 4718592 | tf_op jit(solution)/shard_map/project_and_share/pallas_call | solution.py:623
  156.6 1.2 copy.11
  157.7 1.1 copy.13
Async XLA Ops:
  0.6 126.6 %copy-start = (bf16[128,6144]{1,0:T(8,128)(2,1)S(1)}, bf16[128,6144]{1,0:T(8,128)(2,1)}, u32[]{:S(2)}) copy-start(bf16[128,6144]{1,0:T(8,128)(2,1)} %position_ref.3) | copy-start | bytes 4718596
  127.2 1.2 copy-start.1
  128.4 1.3 copy-start.2

commit v4 on v3

--- a/solution.py
+++ b/solution.py
@@ -155,6 +155,29 @@
                 def _():
                     self.copy(hop, side, source, target).start()
 
+    def rest_copy(self, side, source, target):
+        there = self.slot(source).at[:, self.second]
+        return remote(
+            there, there, self.rest_send.at[side], self.rest_recv.at[side], "mp", target
+        )
+
+    def rest(self):
+        for side, source, target, _, onward in self.ways(self.size - 2):
+            @pl.when(onward)
+            def _():
+                self.rest_copy(side, source, target).start()
+
+    def finish_rest(self):
+        for side, source, target, held, _ in self.ways(self.size - 1):
+            @pl.when(held)
+            def _():
+                self.rest_copy(side, source, target).wait_recv()
+
+        for side, source, target, _, onward in self.ways(self.size - 2):
+            @pl.when(onward)
+            def _():
+                self.rest_copy(side, source, target).wait_send()
+
     def finish(self):
         for hop in range(self.size - 1):
             for side, source, target, _, onward in self.ways(hop):
@@ -168,7 +191,7 @@
     qkv_ref, out_weight_ref, held_ref, columns_ref, copies_ref,
     raised, pixels, blocks, embedded, means, squares, normed, weights, projected, outgoing,
     z_send, z_recv, w_send, w_recv, w_half, h_send, h_recv, g_send, g_recv, g_half,
-    o_send, o_recv, c_send, c_recv, load_sem, own_sem,
+    o_send, o_recv, r_send, r_recv, c_send, c_recv, load_sem, own_sem,
 ):
     me = lax.axis_index("dp")
     here = lax.axis_index("mp")
@@ -217,8 +240,11 @@
     )
     gather.start()
     part = panel_width(width)
-    early = pl.ds(0, width - part)
+    apart = late_panel(nm) and width // part > 2
+    early = pl.ds(0, width - (2 if apart else 1) * part)
     line = Line(nm, own_columns, lambda s: columns_ref.at[s], early, o_send, o_recv)
+    line.second = pl.ds(width - 2 * part, part)
+    line.rest_send, line.rest_recv = r_send, r_recv
     line.hop(0)
     for step in range(1, nm):
         source = lax.rem(here + step, nm)
@@ -391,6 +417,8 @@
 
     last = pairs - 1
     share(last)
+    if apart and nm <= 4:
+        line.rest()
     if last >= 1:
         pass_far(last - 1)
     pass_near(last)
@@ -400,6 +428,10 @@
         copy.wait()
     for hop in range(3, nm + 1):
         line.hop(hop)
+    if apart:
+        if nm > 4:
+            line.rest()
+        line.finish_rest()
     line.finish()
     for step in range(1, nm):
         pixel_copy(step).wait_send()
@@ -596,7 +628,7 @@
             DMA((sends(nd),)), DMA((nd,)), DMA((2,)),
             DMA((pairs, nm)), DMA((pairs, nm)),
             DMA((pairs, sends(nd))), DMA((pairs, nd)), DMA((pairs, 2)),
-            DMA((nm, 2)), DMA((nm,)),
+            DMA((nm, 2)), DMA((nm,)), DMA((2,)), DMA((2,)),
             DMA((nd,)), DMA((nd,)),
             DMA((3,)), DMA((2 + pairs,)),
         ],

time: 159 us -> 150 us (0.943)
  Pallas kernels: 153 us -> 145 us
    pallas_call x1, Pallas kernels: 127 us -> 117 us  [on_device(): pl.pallas_call(functools.partial(heads_kernel, nd, nm), out_shape=(jax.Sh...]
where the time goes in v4:
time: 150 us
  Pallas kernels  145 us (97%)
  local copies, waits for them, and re-layouts  4.78 us (3%)
    pallas_call x1, Pallas kernels, on_device(): pl.pallas_call(functools.partial(heads_kernel, nd, nm), out_shape=(jax.Sh...  117 us
    pallas_call x1, Pallas kernels, on_device(): pl.pallas_call(functools.partial(output_kernel, nd, nm), out_shape=(jax.S...  27.8 us
    unnamed x8, local copies, waits for them, and re-layouts  4.78 us

profile of v4, /device:TPU:1, one launch (start us, length us, event | category | flops | bytes accessed | tf_op | source)
XLA Modules:
  0.0 150.3 jit_solution(9994472197884050387)
XLA Ops:
  0.6 0.0 copy-start
  0.6 117.0 %embed_and_heads.1 = (bf16[8,3,4,128,256]{4,3,2,1,0:T(8,128)(2,1)}, bf16[4,768,768]{2,1,0:T(8,128)(2,1)}, bf16[8,128,640]{2,1,0:T(8,128)(2,1)}) custom-call(bf16[588,128]{1,0:T(8,128)(2,1)} %bitcast.11, bf16[588,128]{1,0:T(8,128)(2,1)} %bitcast.12, bf16[588,768]{1,0:T(8,128)(2,1)} %embed_ref.3, bf16[128,6144]{1,0:T(8,128)(2,1)} %position_ref.3, ...), custom_call_target="tpu_custom_call" | custom-call | flops 19327352832 | bytes 28311552 | tf_op jit(solution)/shard_map/embed_and_heads/pallas_call | solution.py:607
  117.7 0.0 copy-done
  117.7 0.0 copy-start.1
  117.7 1.2 copy-done.1
  118.9 0.0 copy-start.2
  118.9 1.3 copy-done.2
  120.2 27.8 %project_and_share.1 = (bf16[128,6144]{1,0:T(8,128)(2,1)S(1)}, f32[128,768]{1,0:T(8,128)S(1)}) custom-call(bf16[8,3,4,128,256]{4,3,2,1,0:T(8,128)(2,1)} %get-tuple-element.7.heads_ref, bf16[8,128,640]{2,1,0:T(8,128)(2,1)S(1)} %copy-done.2, bf16[588,768]{1,0:T(8,128)(2,1)S(1)} %copy-done.1, bf16[128,6144]{1,0:T(8,128)(2,1)S(1)} %copy-done, ...), custom_call_target="tpu_custom_call" | custom-call | flops 4831838208 | bytes 4718592 | tf_op jit(solution)/shard_map/project_and_share/pallas_call | solution.py:655
  148.0 1.2 copy.11
  149.1 1.1 copy.13
Async XLA Ops:
  0.6 117.0 %copy-start = (bf16[128,6144]{1,0:T(8,128)(2,1)S(1)}, bf16[128,6144]{1,0:T(8,128)(2,1)}, u32[]{:S(2)}) copy-start(bf16[128,6144]{1,0:T(8,128)(2,1)} %position_ref.3) | copy-start | bytes 4718596
  117.7 1.2 copy-start.1
  118.9 1.3 copy-start.2
